TPU v7x, 256 devices: a whole 4x4x8 slice. The times are simulated.
256 devices in a mesh: section: 16 (over x_hi, z), fsdp: 16 (over x_lo, y, core).
Axes of the slice: x: 4 (x_hi: 2, x_lo: 2; x = x_hi * 2 + x_lo), y: 4, z: 8, core: 2. Of those that a mesh axis runs over, the one named last changes fastest.
Arguments:
- acts: bfloat16 [16, 9216, 2048], P('section', 'fsdp'), may hold values from -6 to 6
- gains: float32 [16, 2048], P('section'), may hold values from 0.5 to 1.5
- proj: bfloat16 [16, 2048, 2048], P('section', 'fsdp'), may hold values from -0.0625 to 0.0625
- head: bfloat16 [2048, 512], replicated, may hold values from -1 to 1
- segs: int32 [48, 192], P('fsdp'), may hold values from 0 to 15, never falling along the last dimension, each value on 1 to 24 neighbouring positions
- labels: int32 [48, 16], P('fsdp'), may hold values from 0 to 511
Outputs:
- din: bfloat16 [16, 9216, 2048], P('section', 'fsdp')
- dproj: bfloat16 [16, 2048, 2048], P('section', 'fsdp')
- dgain: float32 [16, 2048], P('section')
Inputs may be any that keep to these rules, and one draw needn't show every extreme that they name: `segs`: each row lists the candidates of one microbatch in order, every candidate has at least one token and one has 24.
All inputs are finite; a program needn't handle non-finite values.
Results may differ from a plain program's by a relative error of at most 0.04.
Values may be sent and summed in bfloat16 or wider, within the bound.
No kernel may reach another device: no remote copies, remote signals or barrier semaphores. Data moves between devices by JAX's collectives and lax.ppermute only.
A program may use at most 128 MiB of HBM per device.

v0:
```python
import jax
import jax.numpy as jnp
from jax import lax
from jax.sharding import PartitionSpec as P

norm_eps = 1e-06


def from_behind(value, axis, by):
    length = lax.axis_size(axis)
    pairs = [(i, i + by) for i in range(length) if 0 <= i + by < length]
    return lax.ppermute(value, axis, pairs)


def per_device(acts, gains, proj, head, segs, labels):
    layer_in = acts[0]
    gain = gains[0]
    sections = lax.axis_size("section")
    section_pos = lax.axis_index("section")
    batches, rows = segs.shape
    width = layer_in.shape[1]
    cands = labels.shape[1]
    classes = head.shape[1]
    weight = lax.all_gather(proj[0], "fsdp", axis=0, tiled=True)
    x_float = layer_in.astype(jnp.float32)
    inv_rms = lax.rsqrt(jnp.mean(x_float * x_float, -1, keepdims=True) + norm_eps)
    x_hat = x_float * inv_rms
    normed = (x_hat * gain).astype(jnp.bfloat16)
    onehot = (segs[:, None, :] == jnp.arange(cands, dtype=jnp.int32)[None, :, None]).astype(
        jnp.float32
    )
    counts = jnp.sum(onehot, -1)

    def top_grad(unused):
        y_top = x_float + jnp.dot(normed, weight, preferred_element_type=jnp.float32)
        y_blocks = y_top.reshape(batches, rows, width)
        pooled = (jnp.einsum("mcr,mrd->mcd", onehot, y_blocks) / counts[..., None]).astype(
            jnp.bfloat16
        )
        logits = jnp.dot(pooled.reshape(-1, width), head, preferred_element_type=jnp.float32)
        target = (
            labels.reshape(-1)[:, None] == jnp.arange(classes, dtype=jnp.int32)[None, :]
        ).astype(jnp.float32)
        dlogit = (jax.nn.sigmoid(logits) - target).astype(jnp.bfloat16)
        dpool = jnp.dot(dlogit, head.T, preferred_element_type=jnp.float32).reshape(
            batches, cands, width
        )
        dpool = dpool / counts[..., None]
        return jnp.einsum("mcr,mcd->mrd", onehot, dpool).astype(jnp.bfloat16)

    def no_grad(unused):
        return jnp.zeros((batches, rows, width), jnp.bfloat16)

    top_grads = lax.cond(section_pos == sections - 1, top_grad, no_grad, 0)
    hat_blocks = x_hat.reshape(batches, rows, width)
    rms_blocks = inv_rms.reshape(batches, rows, 1)

    def backward_one(carry, mb_index, grad_in):
        grads, din, gain_acc, acc, sent = carry
        hat_piece = lax.dynamic_index_in_dim(hat_blocks, mb_index, 0, False)
        rms_piece = lax.dynamic_index_in_dim(rms_blocks, mb_index, 0, False)
        back = lax.dot_general(
            grad_in, weight, (((1,), (1,)), ((), ())), preferred_element_type=jnp.float32
        )
        scaled = back * gain
        through = rms_piece * (scaled - hat_piece * jnp.mean(scaled * hat_piece, -1, keepdims=True))
        layer_grad = (grad_in.astype(jnp.float32) + through).astype(jnp.bfloat16)
        grads = lax.dynamic_update_index_in_dim(grads, grad_in, mb_index, 0)
        din = lax.dynamic_update_index_in_dim(din, layer_grad, mb_index, 0)
        gain_acc = gain_acc + jnp.sum(back * hat_piece, 0)
        return (grads, din, gain_acc, acc, layer_grad)

    def chain_step(step, carry):
        incoming = from_behind(carry[4], "section", -1)
        mbatch = step - (sections - 1 - section_pos)
        active = (mbatch >= 0) & (mbatch < batches)
        mb_index = jnp.clip(mbatch, 0, batches - 1)
        own_top = lax.dynamic_index_in_dim(top_grads, mb_index, 0, False)
        grad_in = jnp.where(section_pos == sections - 1, own_top, incoming)

        def waiting(state):
            return state

        return lax.cond(
            active, lambda state: backward_one(state, mb_index, grad_in), waiting, carry
        )

    acc_shape = (1, 1)
    start = (
        jnp.zeros((batches, rows, width), jnp.bfloat16),
        jnp.zeros((batches, rows, width), jnp.bfloat16),
        jnp.zeros((width,), jnp.float32),
        jnp.zeros(acc_shape, jnp.float32),
        jnp.zeros((rows, width), jnp.bfloat16),
    )
    grads, din, gain_acc, acc, sent = lax.fori_loop(0, sections + batches - 1, chain_step, start)
    gain_total = lax.psum(gain_acc, "fsdp")
    flat_grads = grads.reshape(-1, width)
    weight_part = lax.psum_scatter(
        lax.dot_general(
            normed, flat_grads, (((0,), (0,)), ((), ())), preferred_element_type=jnp.float32
        ).astype(jnp.bfloat16),
        "fsdp",
        scatter_dimension=0,
        tiled=True,
    )
    return (din.reshape(1, -1, width), weight_part[None], gain_total[None])


def solution(mesh):
    return jax.shard_map(
        per_device,
        mesh=mesh,
        in_specs=(
            P("section", "fsdp", None),
            P("section", None),
            P("section", "fsdp", None),
            P(),
            P("fsdp", None),
            P("fsdp", None),
        ),
        out_specs=(P("section", "fsdp", None), P("section", "fsdp", None), P("section", None)),
        check_vma=False,
    )
```

profile of v0, /device:TPU:32, one launch (start us, length us, event | category | flops | bytes accessed | tf_op | source)
XLA Modules:
  0.0 701.0 jit_solution(4104904293156003844)
XLA Ops:
  17.7 49.5 %all-gather.3.cloned.1.call-done = bf16[1,2048,2048]{2,1,0:T(8,128)(2,1)} async-done(((bf16[1,128,2048]{2,1,0:T(8,128)(2,1)}), bf16[1,2048,2048]{2,1,0:T(8,128)(2,1)}) %all-gather.3.cloned.1.call-update) | async-done | bytes 8388624 | tf_op jit(solution)/shard_map/all_gather | solution.py:24
  73.2 527.3 %while.21 = (s32[]{:T(128)}, bf16[3,192,2048]{2,1,0:T(8,128)(2,1)}, bf16[3,192,2048]{2,1,0:T(8,128)(2,1)}, f32[2048]{0:T(1024)S(1)}, bf16[192,2048]{1,0:T(8,128)...) while((s32[]{:T(128)}, bf16[3,192,2048]{2,1,0:T(8,128)(2,1)}, ...), condition=%wide.region_9.10_spmd, body=%wide.region_4.9_spmd.sunk | while | flops 1615724544 | bytes 24172716 | solution.py:96
  75.6 19.4 %collective-permute-done = bf16[192,2048]{1,0:T(8,128)(2,1)S(1)} collective-permute-done((bf16[192,2048]{1,0:T(8,128)(2,1)}, bf16[192,2048]{1,0:T(8,128)(2,1)S(1)}, u32[]{:S(2)}, u32[]{:S(2)}) %collective-permute-start) | collective-permute-done | bytes 786464 | tf_op jit(solution)/shard_map/while/body/eval_jaxpr/ppermute | solution.py:12
  97.4 18.6 %collective-permute-done = bf16[192,2048]{1,0:T(8,128)(2,1)S(1)} collective-permute-done((bf16[192,2048]{1,0:T(8,128)(2,1)}, bf16[192,2048]{1,0:T(8,128)(2,1)S(1)}, u32[]{:S(2)}, u32[]{:S(2)}) %collective-permute-start) | collective-permute-done | bytes 786464 | tf_op jit(solution)/shard_map/while/body/eval_jaxpr/ppermute | solution.py:12
  118.4 18.8 %collective-permute-done = bf16[192,2048]{1,0:T(8,128)(2,1)S(1)} collective-permute-done((bf16[192,2048]{1,0:T(8,128)(2,1)}, bf16[192,2048]{1,0:T(8,128)(2,1)S(1)}, u32[]{:S(2)}, u32[]{:S(2)}) %collective-permute-start) | collective-permute-done | bytes 786464 | tf_op jit(solution)/shard_map/while/body/eval_jaxpr/ppermute | solution.py:12
  139.1 18.4 %collective-permute-done = bf16[192,2048]{1,0:T(8,128)(2,1)S(1)} collective-permute-done((bf16[192,2048]{1,0:T(8,128)(2,1)}, bf16[192,2048]{1,0:T(8,128)(2,1)S(1)}, u32[]{:S(2)}, u32[]{:S(2)}) %collective-permute-start) | collective-permute-done | bytes 786464 | tf_op jit(solution)/shard_map/while/body/eval_jaxpr/ppermute | solution.py:12
  159.4 17.5 %collective-permute-done = bf16[192,2048]{1,0:T(8,128)(2,1)S(1)} collective-permute-done((bf16[192,2048]{1,0:T(8,128)(2,1)}, bf16[192,2048]{1,0:T(8,128)(2,1)S(1)}, u32[]{:S(2)}, u32[]{:S(2)}) %collective-permute-start) | collective-permute-done | bytes 786464 | tf_op jit(solution)/shard_map/while/body/eval_jaxpr/ppermute | solution.py:12
  178.9 16.6 %collective-permute-done = bf16[192,2048]{1,0:T(8,128)(2,1)S(1)} collective-permute-done((bf16[192,2048]{1,0:T(8,128)(2,1)}, bf16[192,2048]{1,0:T(8,128)(2,1)S(1)}, u32[]{:S(2)}, u32[]{:S(2)}) %collective-permute-start) | collective-permute-done | bytes 786464 | tf_op jit(solution)/shard_map/while/body/eval_jaxpr/ppermute | solution.py:12
  197.4 15.8 %collective-permute-done = bf16[192,2048]{1,0:T(8,128)(2,1)S(1)} collective-permute-done((bf16[192,2048]{1,0:T(8,128)(2,1)}, bf16[192,2048]{1,0:T(8,128)(2,1)S(1)}, u32[]{:S(2)}, u32[]{:S(2)}) %collective-permute-start) | collective-permute-done | bytes 786464 | tf_op jit(solution)/shard_map/while/body/eval_jaxpr/ppermute | solution.py:12
  215.1 14.8 %collective-permute-done = bf16[192,2048]{1,0:T(8,128)(2,1)S(1)} collective-permute-done((bf16[192,2048]{1,0:T(8,128)(2,1)}, bf16[192,2048]{1,0:T(8,128)(2,1)S(1)}, u32[]{:S(2)}, u32[]{:S(2)}) %collective-permute-start) | collective-permute-done | bytes 786464 | tf_op jit(solution)/shard_map/while/body/eval_jaxpr/ppermute | solution.py:12
  232.3 17.2 %collective-permute-done = bf16[192,2048]{1,0:T(8,128)(2,1)S(1)} collective-permute-done((bf16[192,2048]{1,0:T(8,128)(2,1)}, bf16[192,2048]{1,0:T(8,128)(2,1)S(1)}, u32[]{:S(2)}, u32[]{:S(2)}) %collective-permute-start) | collective-permute-done | bytes 786464 | tf_op jit(solution)/shard_map/while/body/eval_jaxpr/ppermute | solution.py:12
  251.4 15.8 %collective-permute-done = bf16[192,2048]{1,0:T(8,128)(2,1)S(1)} collective-permute-done((bf16[192,2048]{1,0:T(8,128)(2,1)}, bf16[192,2048]{1,0:T(8,128)(2,1)S(1)}, u32[]{:S(2)}, u32[]{:S(2)}) %collective-permute-start) | collective-permute-done | bytes 786464 | tf_op jit(solution)/shard_map/while/body/eval_jaxpr/ppermute | solution.py:12
  269.1 16.1 %collective-permute-done = bf16[192,2048]{1,0:T(8,128)(2,1)S(1)} collective-permute-done((bf16[192,2048]{1,0:T(8,128)(2,1)}, bf16[192,2048]{1,0:T(8,128)(2,1)S(1)}, u32[]{:S(2)}, u32[]{:S(2)}) %collective-permute-start) | collective-permute-done | bytes 786464 | tf_op jit(solution)/shard_map/while/body/eval_jaxpr/ppermute | solution.py:12
  287.1 16.0 %collective-permute-done = bf16[192,2048]{1,0:T(8,128)(2,1)S(1)} collective-permute-done((bf16[192,2048]{1,0:T(8,128)(2,1)}, bf16[192,2048]{1,0:T(8,128)(2,1)S(1)}, u32[]{:S(2)}, u32[]{:S(2)}) %collective-permute-start) | collective-permute-done | bytes 786464 | tf_op jit(solution)/shard_map/while/body/eval_jaxpr/ppermute | solution.py:12
  305.0 14.9 %collective-permute-done = bf16[192,2048]{1,0:T(8,128)(2,1)S(1)} collective-permute-done((bf16[192,2048]{1,0:T(8,128)(2,1)}, bf16[192,2048]{1,0:T(8,128)(2,1)S(1)}, u32[]{:S(2)}, u32[]{:S(2)}) %collective-permute-start) | collective-permute-done | bytes 786464 | tf_op jit(solution)/shard_map/while/body/eval_jaxpr/ppermute | solution.py:12
  322.0 13.8 %collective-permute-done = bf16[192,2048]{1,0:T(8,128)(2,1)S(1)} collective-permute-done((bf16[192,2048]{1,0:T(8,128)(2,1)}, bf16[192,2048]{1,0:T(8,128)(2,1)S(1)}, u32[]{:S(2)}, u32[]{:S(2)}) %collective-permute-start) | collective-permute-done | bytes 786464 | tf_op jit(solution)/shard_map/while/body/eval_jaxpr/ppermute | solution.py:12
  337.7 178.5 %collective-permute-done = bf16[192,2048]{1,0:T(8,128)(2,1)S(1)} collective-permute-done((bf16[192,2048]{1,0:T(8,128)(2,1)}, bf16[192,2048]{1,0:T(8,128)(2,1)S(1)}, u32[]{:S(2)}, u32[]{:S(2)}) %collective-permute-start) | collective-permute-done | bytes 786464 | tf_op jit(solution)/shard_map/while/body/eval_jaxpr/ppermute | solution.py:12
  516.3 12.3 %conditional.4 = ((bf16[3,192,2048]{2,1,0:T(8,128)(2,1)}, bf16[3,192,2048]{2,1,0:T(8,128)(2,1)}, f32[2048]{0:T(1024)S(1)}, bf16[192,2048]{1,0:T(8,128)(2,1)})) conditional(s32[]{:T(128)} %convert_element_type.116, (bf16[3,192,2048]{2,1,0:T(8,128)(2,1)}, bf16[3,192,2048]{2,1,0:T(8,128)(2,1)}, f32[2048]{0:T(1024)S(1)}, ...), branch_computations={%region_5.5_spmd, %region_6.8_spmd} | conditional | flops 1615724544 | bytes 21026640 | solution.py:84
  530.5 14.5 %collective-permute-done = bf16[192,2048]{1,0:T(8,128)(2,1)S(1)} collective-permute-done((bf16[192,2048]{1,0:T(8,128)(2,1)}, bf16[192,2048]{1,0:T(8,128)(2,1)S(1)}, u32[]{:S(2)}, u32[]{:S(2)}) %collective-permute-start) | collective-permute-done | bytes 786464 | tf_op jit(solution)/shard_map/while/body/eval_jaxpr/ppermute | solution.py:12
  545.0 12.2 %conditional.4 = ((bf16[3,192,2048]{2,1,0:T(8,128)(2,1)}, bf16[3,192,2048]{2,1,0:T(8,128)(2,1)}, f32[2048]{0:T(1024)S(1)}, bf16[192,2048]{1,0:T(8,128)(2,1)})) conditional(s32[]{:T(128)} %convert_element_type.116, (bf16[3,192,2048]{2,1,0:T(8,128)(2,1)}, bf16[3,192,2048]{2,1,0:T(8,128)(2,1)}, f32[2048]{0:T(1024)S(1)}, ...), branch_computations={%region_5.5_spmd, %region_6.8_spmd} | conditional | flops 1615724544 | bytes 21026640 | solution.py:84
  559.1 15.0 %collective-permute-done = bf16[192,2048]{1,0:T(8,128)(2,1)S(1)} collective-permute-done((bf16[192,2048]{1,0:T(8,128)(2,1)}, bf16[192,2048]{1,0:T(8,128)(2,1)S(1)}, u32[]{:S(2)}, u32[]{:S(2)}) %collective-permute-start) | collective-permute-done | bytes 786464 | tf_op jit(solution)/shard_map/while/body/eval_jaxpr/ppermute | solution.py:12
  574.1 12.2 %conditional.4 = ((bf16[3,192,2048]{2,1,0:T(8,128)(2,1)}, bf16[3,192,2048]{2,1,0:T(8,128)(2,1)}, f32[2048]{0:T(1024)S(1)}, bf16[192,2048]{1,0:T(8,128)(2,1)})) conditional(s32[]{:T(128)} %convert_element_type.116, (bf16[3,192,2048]{2,1,0:T(8,128)(2,1)}, bf16[3,192,2048]{2,1,0:T(8,128)(2,1)}, f32[2048]{0:T(1024)S(1)}, ...), branch_computations={%region_5.5_spmd, %region_6.8_spmd} | conditional | flops 1615724544 | bytes 21026640 | solution.py:84
  611.3 28.3 %psum.7 = f32[1,2048]{1,0:T(1,128)} all-reduce(f32[1,2048]{1,0:T(1,128)S(1)} %bitcast.65), channel_id=1, replica_groups=mesh['section'=16,'fsdp'=16] {'fsdp'}, use_global_device_ids=true, to_apply=%region_11.12 | all-reduce | flops 2048 | bytes 16384 | tf_op jit(solution)/shard_map/psum | solution.py:97
  639.6 54.5 %reduce-scatter.2.cloned.1.call-done = bf16[128,2048]{1,0:T(8,128)(2,1)} async-done(((bf16[2048,2048]{1,0:T(8,128)(2,1)}), bf16[128,2048]{1,0:T(8,128)(2,1)}) %reduce-scatter.2.cloned.1.call-update) | async-done | bytes 524304 | tf_op jit(solution)/shard_map/reduce_scatter | solution.py:99
  (79 shorter events, 114.2 us)
Async XLA Ops:
  7.2 3.2 copy-start
  7.2 3.2 copy-start.2
  7.2 3.2 copy-start.1
  7.2 60.0 %all-gather.3.cloned.1.call-start = ((), (), s32[]{:S(2)}) async-start(), calls=%async_computation.2 | async-start | bytes 8912896 | tf_op jit(solution)/shard_map/all_gather | solution.py:24
  7.9 686.2 %reduce-scatter.2.cloned.1.call-start = ((), (), s32[]{:S(2)}) async-start(), calls=%async_computation.1 | async-start | bytes 8912896 | tf_op jit(solution)/shard_map/reduce_scatter | solution.py:99
  15.1 52.0 %copy-start.3 = (s32[3,16]{1,0:T(4,128)S(1)}, s32[3,16]{1,0:T(4,128)}, u32[]{:S(2)}) copy-start(s32[3,16]{1,0:T(4,128)} %param.17) | copy-start | bytes 580
  73.2 21.8 %collective-permute-start = (bf16[192,2048]{1,0:T(8,128)(2,1)}, bf16[192,2048]{1,0:T(8,128)(2,1)S(1)}, u32[]{:S(2)}, u32[]{:S(2)}) collective-permute-start(bf16[192,2048]{1,0:T(8,128)(2,1)} %get-tuple-element.576), channel_id=1, source_target_pairs={{16,0},{32,16},{48,32},{64,48},{80,64},{96,80},{112,96},{128,112},... | collective-permute-start | bytes 2359304 | tf_op jit(solution)/shard_map/while/body/eval_jaxpr/ppermute | solution.py:12
  95.0 21.0 %collective-permute-start = (bf16[192,2048]{1,0:T(8,128)(2,1)}, bf16[192,2048]{1,0:T(8,128)(2,1)S(1)}, u32[]{:S(2)}, u32[]{:S(2)}) collective-permute-start(bf16[192,2048]{1,0:T(8,128)(2,1)} %get-tuple-element.576), channel_id=1, source_target_pairs={{16,0},{32,16},{48,32},{64,48},{80,64},{96,80},{112,96},{128,112},... | collective-permute-start | bytes 2359304 | tf_op jit(solution)/shard_map/while/body/eval_jaxpr/ppermute | solution.py:12
  116.0 21.2 %collective-permute-start = (bf16[192,2048]{1,0:T(8,128)(2,1)}, bf16[192,2048]{1,0:T(8,128)(2,1)S(1)}, u32[]{:S(2)}, u32[]{:S(2)}) collective-permute-start(bf16[192,2048]{1,0:T(8,128)(2,1)} %get-tuple-element.576), channel_id=1, source_target_pairs={{16,0},{32,16},{48,32},{64,48},{80,64},{96,80},{112,96},{128,112},... | collective-permute-start | bytes 2359304 | tf_op jit(solution)/shard_map/while/body/eval_jaxpr/ppermute | solution.py:12
  137.2 20.3 %collective-permute-start = (bf16[192,2048]{1,0:T(8,128)(2,1)}, bf16[192,2048]{1,0:T(8,128)(2,1)S(1)}, u32[]{:S(2)}, u32[]{:S(2)}) collective-permute-start(bf16[192,2048]{1,0:T(8,128)(2,1)} %get-tuple-element.576), channel_id=1, source_target_pairs={{16,0},{32,16},{48,32},{64,48},{80,64},{96,80},{112,96},{128,112},... | collective-permute-start | bytes 2359304 | tf_op jit(solution)/shard_map/while/body/eval_jaxpr/ppermute | solution.py:12
  157.5 19.4 %collective-permute-start = (bf16[192,2048]{1,0:T(8,128)(2,1)}, bf16[192,2048]{1,0:T(8,128)(2,1)S(1)}, u32[]{:S(2)}, u32[]{:S(2)}) collective-permute-start(bf16[192,2048]{1,0:T(8,128)(2,1)} %get-tuple-element.576), channel_id=1, source_target_pairs={{16,0},{32,16},{48,32},{64,48},{80,64},{96,80},{112,96},{128,112},... | collective-permute-start | bytes 2359304 | tf_op jit(solution)/shard_map/while/body/eval_jaxpr/ppermute | solution.py:12
  176.9 18.5 %collective-permute-start = (bf16[192,2048]{1,0:T(8,128)(2,1)}, bf16[192,2048]{1,0:T(8,128)(2,1)S(1)}, u32[]{:S(2)}, u32[]{:S(2)}) collective-permute-start(bf16[192,2048]{1,0:T(8,128)(2,1)} %get-tuple-element.576), channel_id=1, source_target_pairs={{16,0},{32,16},{48,32},{64,48},{80,64},{96,80},{112,96},{128,112},... | collective-permute-start | bytes 2359304 | tf_op jit(solution)/shard_map/while/body/eval_jaxpr/ppermute | solution.py:12
  195.4 17.7 %collective-permute-start = (bf16[192,2048]{1,0:T(8,128)(2,1)}, bf16[192,2048]{1,0:T(8,128)(2,1)S(1)}, u32[]{:S(2)}, u32[]{:S(2)}) collective-permute-start(bf16[192,2048]{1,0:T(8,128)(2,1)} %get-tuple-element.576), channel_id=1, source_target_pairs={{16,0},{32,16},{48,32},{64,48},{80,64},{96,80},{112,96},{128,112},... | collective-permute-start | bytes 2359304 | tf_op jit(solution)/shard_map/while/body/eval_jaxpr/ppermute | solution.py:12
  213.1 16.7 %collective-permute-start = (bf16[192,2048]{1,0:T(8,128)(2,1)}, bf16[192,2048]{1,0:T(8,128)(2,1)S(1)}, u32[]{:S(2)}, u32[]{:S(2)}) collective-permute-start(bf16[192,2048]{1,0:T(8,128)(2,1)} %get-tuple-element.576), channel_id=1, source_target_pairs={{16,0},{32,16},{48,32},{64,48},{80,64},{96,80},{112,96},{128,112},... | collective-permute-start | bytes 2359304 | tf_op jit(solution)/shard_map/while/body/eval_jaxpr/ppermute | solution.py:12
  229.9 19.6 %collective-permute-start = (bf16[192,2048]{1,0:T(8,128)(2,1)}, bf16[192,2048]{1,0:T(8,128)(2,1)S(1)}, u32[]{:S(2)}, u32[]{:S(2)}) collective-permute-start(bf16[192,2048]{1,0:T(8,128)(2,1)} %get-tuple-element.576), channel_id=1, source_target_pairs={{16,0},{32,16},{48,32},{64,48},{80,64},{96,80},{112,96},{128,112},... | collective-permute-start | bytes 2359304 | tf_op jit(solution)/shard_map/while/body/eval_jaxpr/ppermute | solution.py:12
  249.5 17.7 %collective-permute-start = (bf16[192,2048]{1,0:T(8,128)(2,1)}, bf16[192,2048]{1,0:T(8,128)(2,1)S(1)}, u32[]{:S(2)}, u32[]{:S(2)}) collective-permute-start(bf16[192,2048]{1,0:T(8,128)(2,1)} %get-tuple-element.576), channel_id=1, source_target_pairs={{16,0},{32,16},{48,32},{64,48},{80,64},{96,80},{112,96},{128,112},... | collective-permute-start | bytes 2359304 | tf_op jit(solution)/shard_map/while/body/eval_jaxpr/ppermute | solution.py:12
  267.2 18.0 %collective-permute-start = (bf16[192,2048]{1,0:T(8,128)(2,1)}, bf16[192,2048]{1,0:T(8,128)(2,1)S(1)}, u32[]{:S(2)}, u32[]{:S(2)}) collective-permute-start(bf16[192,2048]{1,0:T(8,128)(2,1)} %get-tuple-element.576), channel_id=1, source_target_pairs={{16,0},{32,16},{48,32},{64,48},{80,64},{96,80},{112,96},{128,112},... | collective-permute-start | bytes 2359304 | tf_op jit(solution)/shard_map/while/body/eval_jaxpr/ppermute | solution.py:12
  285.2 17.9 %collective-permute-start = (bf16[192,2048]{1,0:T(8,128)(2,1)}, bf16[192,2048]{1,0:T(8,128)(2,1)S(1)}, u32[]{:S(2)}, u32[]{:S(2)}) collective-permute-start(bf16[192,2048]{1,0:T(8,128)(2,1)} %get-tuple-element.576), channel_id=1, source_target_pairs={{16,0},{32,16},{48,32},{64,48},{80,64},{96,80},{112,96},{128,112},... | collective-permute-start | bytes 2359304 | tf_op jit(solution)/shard_map/while/body/eval_jaxpr/ppermute | solution.py:12
  303.1 16.9 %collective-permute-start = (bf16[192,2048]{1,0:T(8,128)(2,1)}, bf16[192,2048]{1,0:T(8,128)(2,1)S(1)}, u32[]{:S(2)}, u32[]{:S(2)}) collective-permute-start(bf16[192,2048]{1,0:T(8,128)(2,1)} %get-tuple-element.576), channel_id=1, source_target_pairs={{16,0},{32,16},{48,32},{64,48},{80,64},{96,80},{112,96},{128,112},... | collective-permute-start | bytes 2359304 | tf_op jit(solution)/shard_map/while/body/eval_jaxpr/ppermute | solution.py:12
  319.9 15.9 %collective-permute-start = (bf16[192,2048]{1,0:T(8,128)(2,1)}, bf16[192,2048]{1,0:T(8,128)(2,1)S(1)}, u32[]{:S(2)}, u32[]{:S(2)}) collective-permute-start(bf16[192,2048]{1,0:T(8,128)(2,1)} %get-tuple-element.576), channel_id=1, source_target_pairs={{16,0},{32,16},{48,32},{64,48},{80,64},{96,80},{112,96},{128,112},... | collective-permute-start | bytes 2359304 | tf_op jit(solution)/shard_map/while/body/eval_jaxpr/ppermute | solution.py:12
  335.8 180.5 %collective-permute-start = (bf16[192,2048]{1,0:T(8,128)(2,1)}, bf16[192,2048]{1,0:T(8,128)(2,1)S(1)}, u32[]{:S(2)}, u32[]{:S(2)}) collective-permute-start(bf16[192,2048]{1,0:T(8,128)(2,1)} %get-tuple-element.576), channel_id=1, source_target_pairs={{16,0},{32,16},{48,32},{64,48},{80,64},{96,80},{112,96},{128,112},... | collective-permute-start | bytes 2359304 | tf_op jit(solution)/shard_map/while/body/eval_jaxpr/ppermute | solution.py:12
  528.5 16.4 %collective-permute-start = (bf16[192,2048]{1,0:T(8,128)(2,1)}, bf16[192,2048]{1,0:T(8,128)(2,1)S(1)}, u32[]{:S(2)}, u32[]{:S(2)}) collective-permute-start(bf16[192,2048]{1,0:T(8,128)(2,1)} %get-tuple-element.576), channel_id=1, source_target_pairs={{16,0},{32,16},{48,32},{64,48},{80,64},{96,80},{112,96},{128,112},... | collective-permute-start | bytes 2359304 | tf_op jit(solution)/shard_map/while/body/eval_jaxpr/ppermute | solution.py:12
  557.2 16.9 %collective-permute-start = (bf16[192,2048]{1,0:T(8,128)(2,1)}, bf16[192,2048]{1,0:T(8,128)(2,1)S(1)}, u32[]{:S(2)}, u32[]{:S(2)}) collective-permute-start(bf16[192,2048]{1,0:T(8,128)(2,1)} %get-tuple-element.576), channel_id=1, source_target_pairs={{16,0},{32,16},{48,32},{64,48},{80,64},{96,80},{112,96},{128,112},... | collective-permute-start | bytes 2359304 | tf_op jit(solution)/shard_map/while/body/eval_jaxpr/ppermute | solution.py:12
  586.4 14.1 %collective-permute-start = (bf16[192,2048]{1,0:T(8,128)(2,1)}, bf16[192,2048]{1,0:T(8,128)(2,1)S(1)}, u32[]{:S(2)}, u32[]{:S(2)}) collective-permute-start(bf16[192,2048]{1,0:T(8,128)(2,1)} %get-tuple-element.576), channel_id=1, source_target_pairs={{16,0},{32,16},{48,32},{64,48},{80,64},{96,80},{112,96},{128,112},... | collective-permute-start | bytes 2359304 | tf_op jit(solution)/shard_map/while/body/eval_jaxpr/ppermute | solution.py:12
Sparse Core Ops, SparseCore 0:
  9.9 57.2 all-gather.2
  611.4 82.6 reduce-scatter.1
where the time goes:
time: 702 us; the launch traced here: 701 us
  waiting for transfers between devices  559 us (80%)
  starting transfers between devices  36.5 us (5%)
  matrix products  31.3 us (4%)
  blocking collectives  28.3 us (4%)
  other arithmetic  25.6 us (4%)
  between operations  14.1 us (2%)
    ppermute x18, waiting for transfers between devices, from_behind(): return lax.ppermute(value, axis, pairs)  454 us
    reduce_scatter x1, waiting for transfers between devices, per_device(): lax.psum_scatter(lax.dot_general(normed, flat_grads, (((0,), (0,)), ((),...  54.5 us
    all_gather x1, waiting for transfers between devices, per_device(): weight = lax.all_gather(proj[0], 'fsdp', axis=0, tiled=True)  49.5 us
    ppermute x18, starting transfers between devices, from_behind(): return lax.ppermute(value, axis, pairs)  36.4 us
    psum x1, blocking collectives, per_device(): gain_total = lax.psum(gain_acc, 'fsdp')  28.3 us
    dot_general x3, matrix products, backward_one(): lax.dot_general(grad_in, weight, (((1,), (1,)), ((), ())), preferred_elem...  20.5 us
  transfers between devices with their start and end apart: 20, of which 20 were waited for; matrix products, arithmetic and copies ran while one was open for 1% of the time, Pallas kernels for 0%

commit v1 on v0

v1 whole, which is shorter than its diff:
```python
import functools

import jax
import jax.numpy as jnp
from jax import lax
from jax.experimental import pallas as pl
from jax.experimental.pallas import tpu as pltpu
from jax.sharding import PartitionSpec as P

norm_eps = 1e-06
piece = 48
lag = 2


def step_kernel(
    step,
    last,
    place,
    recv,
    weight,
    acts,
    rms,
    gain,
    grads_in,
    din_in,
    acc_in,
    out,
    grads,
    din,
    acc,
):
    rows, width = recv.shape
    index = step - lag * place[0]

    @pl.when((index >= 0) & (index <= last))
    def _():
        row = pl.multiple_of(index * rows, 16)
        here = pl.ds(row, rows)

        @pl.when(place[0] > 0)
        def _():
            grads[here, :] = recv[...]

        grad = grads[here, :]
        back = lax.dot_general(
            grad, weight[...], (((1,), (1,)), ((), ())), preferred_element_type=jnp.float32
        )
        inv_rms = rms[here, :]
        x_hat = acts[here, :].astype(jnp.float32) * inv_rms
        scaled = back * gain[...]
        mean = jnp.sum(scaled * x_hat, -1, keepdims=True) * (1.0 / width)
        layer_grad = (grad.astype(jnp.float32) + inv_rms * (scaled - x_hat * mean)).astype(
            jnp.bfloat16
        )
        out[...] = layer_grad
        din[here, :] = layer_grad
        acc[...] += jnp.sum((back * x_hat).reshape(rows // 8, 8, width), 0)


def in_vmem(value):
    return pltpu.with_memory_space_constraint(value, pltpu.VMEM)


whole = pl.BlockSpec(memory_space=pltpu.VMEM)


def chain_step(step, place, recv, weight, acts, rms, gain, grads, din, acc):
    rows, width = recv.shape
    return pl.pallas_call(
        functools.partial(step_kernel, step, acts.shape[0] // rows - 1),
        out_shape=(
            pltpu.VMEM((rows, width), jnp.bfloat16),
            pltpu.VMEM(grads.shape, grads.dtype),
            pltpu.VMEM(din.shape, din.dtype),
            pltpu.VMEM(acc.shape, acc.dtype),
        ),
        in_specs=[pl.BlockSpec(memory_space=pltpu.SMEM)] + [whole] * 8,
        out_specs=(whole,) * 4,
        input_output_aliases={6: 1, 7: 2, 8: 3},
        compiler_params=pltpu.CompilerParams(vmem_limit_bytes=8 * 2**20),
        cost_estimate=pl.CostEstimate(
            flops=2 * rows * width * width, bytes_accessed=width * width * 2, transcendentals=0
        ),
        name="chain_step",
    )(place, *[in_vmem(v) for v in (recv, weight, acts, rms, gain, grads, din, acc)])


def finish_kernel(normed_t, grads, din, acc, product, din_out, gain_out, slots, sems, din_sem):
    keep = pltpu.make_async_copy(din, din_out, din_sem)
    keep.start()
    gain_out[...] = jnp.sum(acc[...], 0, keepdims=True)
    rows = slots.shape[1]
    copies = []
    for block in range(product.shape[0] // rows):
        slot = block % 2
        if block >= 2:
            copies[block - 2].wait()
        slots[slot] = jnp.dot(
            normed_t[block * rows : (block + 1) * rows, :],
            grads[...],
            preferred_element_type=jnp.float32,
        ).astype(jnp.bfloat16)
        copies.append(
            pltpu.make_async_copy(
                slots.at[slot], product.at[block * rows : (block + 1) * rows, :], sems.at[slot]
            )
        )
        copies[-1].start()
    copies[-2].wait()
    copies[-1].wait()
    keep.wait()


def finish(normed_t, grads, din, acc):
    width, tokens = normed_t.shape
    anywhere = pl.BlockSpec(memory_space=pl.ANY)
    return pl.pallas_call(
        finish_kernel,
        out_shape=(
            pltpu.HBM((width, width), jnp.bfloat16),
            pltpu.HBM((tokens, width), jnp.bfloat16),
            jax.ShapeDtypeStruct((1, width), jnp.float32),
        ),
        in_specs=[whole] * 4,
        out_specs=(anywhere, anywhere, whole),
        scratch_shapes=[
            pltpu.VMEM((2, 256, width), jnp.bfloat16),
            pltpu.SemaphoreType.DMA((2,)),
            pltpu.SemaphoreType.DMA,
        ],
        compiler_params=pltpu.CompilerParams(vmem_limit_bytes=12 * 2**20),
        cost_estimate=pl.CostEstimate(
            flops=2 * tokens * width * width, bytes_accessed=width * width * 2, transcendentals=0
        ),
        name="finish",
    )(*[in_vmem(v) for v in (normed_t, grads, din, acc)])


def top_grads(layer_in, normed, weight, head, segs, labels):
    batches, rows = segs.shape
    width = layer_in.shape[1]
    cands = labels.shape[1]
    classes = head.shape[1]
    onehot = (segs[:, None, :] == jnp.arange(cands, dtype=jnp.int32)[None, :, None]).astype(
        jnp.bfloat16
    )
    counts = jnp.sum(onehot.astype(jnp.float32), -1).reshape(-1, 1)

    def pool(value):
        return jnp.einsum(
            "mcr,mrd->mcd",
            onehot,
            value.reshape(batches, rows, width),
            preferred_element_type=jnp.float32,
        ).reshape(-1, width)

    pooled_normed = pool(normed)
    high = lax.reduce_precision(pooled_normed, 8, 7)
    low = pooled_normed - high
    both = jnp.concatenate([high, low]).astype(jnp.bfloat16)
    product = jnp.dot(both, weight, preferred_element_type=jnp.float32)
    y_pool = pool(layer_in) + product[: batches * cands] + product[batches * cands :]
    pooled = (y_pool / counts).astype(jnp.bfloat16)
    logits = jnp.dot(pooled, head, preferred_element_type=jnp.float32)
    target = (
        labels.reshape(-1)[:, None] == jnp.arange(classes, dtype=jnp.int32)[None, :]
    ).astype(jnp.float32)
    dlogit = (jax.nn.sigmoid(logits) - target).astype(jnp.bfloat16)
    dpool = lax.dot_general(
        dlogit, head, (((1,), (1,)), ((), ())), preferred_element_type=jnp.float32
    )
    cand_grad = (dpool / counts).astype(jnp.bfloat16).reshape(batches, cands, width)
    return (
        jnp.einsum("mcr,mcd->mrd", onehot, cand_grad, preferred_element_type=jnp.float32)
        .astype(jnp.bfloat16)
        .reshape(-1, width)
    )


def per_device(acts, gains, proj, head, segs, labels):
    layer_in = acts[0]
    gain = gains[0]
    sections = lax.axis_size("section")
    section_pos = lax.axis_index("section")
    tokens, width = layer_in.shape
    weight = lax.all_gather(proj[0], "fsdp", axis=0, tiled=True)
    x_float = layer_in.astype(jnp.float32)
    inv_rms = lax.rsqrt(jnp.mean(x_float * x_float, -1, keepdims=True) + norm_eps)
    normed = (x_float * inv_rms * gain).astype(jnp.bfloat16)
    grads = top_grads(layer_in, normed, weight, head, segs, labels)

    pieces = tokens // piece
    place = jnp.reshape(sections - 1 - section_pos, (1,)).astype(jnp.int32)
    din = jnp.zeros((tokens, width), jnp.bfloat16)
    acc = jnp.zeros((8, width), jnp.float32)
    received = {}
    blank = jnp.zeros((piece, width), jnp.bfloat16)
    for step in range(pieces + lag * (sections - 1)):
        out, grads, din, acc = chain_step(
            step,
            place,
            received.pop(step - lag, blank),
            weight,
            layer_in,
            inv_rms,
            gain[None],
            grads,
            din,
            acc,
        )
        pairs = [
            (s, s - 1)
            for s in range(1, sections)
            if 0 <= step - lag * (sections - 1 - s) < pieces
        ]
        if pairs:
            received[step] = lax.ppermute(out, "section", pairs)

    product, din, gain_part = finish(normed.T, grads, din, acc)
    gain_total = lax.psum(gain_part[0], "fsdp")
    weight_part = lax.psum_scatter(product, "fsdp", scatter_dimension=0, tiled=True)
    return (din[None], weight_part[None], gain_total[None])


def solution(mesh):
    return jax.shard_map(
        per_device,
        mesh=mesh,
        in_specs=(
            P("section", "fsdp", None),
            P("section", None),
            P("section", "fsdp", None),
            P(),
            P("fsdp", None),
            P("fsdp", None),
        ),
        out_specs=(P("section", "fsdp", None), P("section", "fsdp", None), P("section", None)),
        check_vma=False,
    )
```

time: 702 us -> 480 us (0.68); the launches traced: 701 us -> 471 us
  waiting for transfers between devices: 559 us -> 183 us
  starting transfers between devices: 36.5 us -> 163 us
  Pallas kernels: 0 us -> 58 us
  other arithmetic: 25.6 us -> 3.3 us
  matrix products: 31.3 us -> 9.75 us
    ppermute x18 -> x40, waiting for transfers between devices: 454 us -> 84.1 us  [per_device(): received[step] = lax.ppermute(out, 'section', pairs)]
    ppermute x18 -> x40, starting transfers between devices: 36.4 us -> 163 us  [per_device(): received[step] = lax.ppermute(out, 'section', pairs)]
    pallas_call x0 -> x43, Pallas kernels: none -> 58 us  [the longest x42 49 us: chain_step(): pl.pallas_call(functools.partial(step_kernel, step, acts.shape[0] // rows...]
    dot_general x4 -> x5, matrix products: 31.3 us -> 9.75 us  [the longest x1 4.87 us: top_grads(): product = jnp.dot(both, weight, preferred_element_type=jnp.float32)]
    dynamic_update_slice x6 -> x0, other arithmetic: 16.1 us -> none  [the longest x3 9.04 us: backward_one(): din = lax.dynamic_update_index_in_dim(din, layer_grad, mb_index, 0)]
    unnamed x8 -> x25, local copies, waits for them, and re-layouts: 0.02 us -> 8.51 us
  transfers between devices with their start and end apart: 20 -> 42, of which waited for: 20 -> 12; matrix products, arithmetic and copies ran while one was open for 1% -> 2% of each run, Pallas kernels for 0% -> 10%
where the time goes in v1:
time: 480 us; the launch traced here: 471 us
  waiting for transfers between devices  183 us (38%)
  starting transfers between devices  163 us (34%)
  Pallas kernels  58 us (12%)
  blocking collectives  28.7 us (6%)
  between operations  15.5 us (3%)
  matrix products  9.75 us (2%)
  local copies, waits for them, and re-layouts  9.18 us (2%)
    ppermute x40, starting transfers between devices, per_device(): received[step] = lax.ppermute(out, 'section', pairs)  163 us
    ppermute x40, waiting for transfers between devices, per_device(): received[step] = lax.ppermute(out, 'section', pairs)  84.1 us
    reduce_scatter x1, waiting for transfers between devices, per_device(): lax.psum_scatter(product, 'fsdp', scatter_dimension=0, tiled=True)  49.9 us
    pallas_call x42, Pallas kernels, chain_step(): pl.pallas_call(functools.partial(step_kernel, step, acts.shape[0] // rows...  49 us
    all_gather x1, waiting for transfers between devices, per_device(): weight = lax.all_gather(proj[0], 'fsdp', axis=0, tiled=True)  48.7 us
    psum x1, blocking collectives, per_device(): gain_total = lax.psum(gain_part[0], 'fsdp')  28.7 us
  transfers between devices with their start and end apart: 42, of which 12 were waited for; matrix products, arithmetic and copies ran while one was open for 2% of the time, Pallas kernels for 10%

profile of v1, /device:TPU:32, one launch (start us, length us, event | category | flops | bytes accessed | tf_op | source)
XLA Modules:
  0.0 471.2 jit_solution(18314402120613742730)
XLA Ops:
  8.0 4.3 copy.178
  18.4 48.7 %all-gather.3.cloned.1.call-done = bf16[1,2048,2048]{2,1,0:T(8,128)(2,1)} async-done(((bf16[1,128,2048]{2,1,0:T(8,128)(2,1)}), bf16[1,2048,2048]{2,1,0:T(8,128)(2,1)}) %all-gather.3.cloned.1.call-update) | async-done | bytes 8388624 | tf_op jit(solution)/shard_map/all_gather | solution.py:186
  67.2 4.9 %fusion.16 = f32[96,2048]{1,0:T(8,128)S(1)} fusion(bf16[48,2048]{1,0:T(8,128)(2,1)S(1)} %get-tuple-element.342, bf16[48,2048]{1,0:T(8,128)(2,1)S(1)} %get-tuple-element.341, bf16[1,2048,2048]{2,1,0:T(8,128)(2,1)} %all-gather.3.cloned.1.call-done), kind=kOutput, calls=%fused_computation.26 | convolution fusion | flops 806092800 | bytes 9568256 | tf_op jit(solution)/shard_map/dot_general | solution.py:161
  75.0 3.4 copy-done.1
  85.7 9.0 %chain_step.52 = (bf16[48,2048]{1,0:T(8,128)(2,1)S(1)}, bf16[576,2048]{1,0:T(8,128)(2,1)S(1)}, bf16[576,2048]{1,0:T(8,128)(2,1)S(1)}, f32[8,2048]{1,0:T(8,128)S(1)}) custom-call(s32[1]{0:T(128)} %bitcast.3.place, bf16[48,2048]{1,0:T(8,128)(2,1)S(1)} %collective-permute-done.9.recv, ...), custom_call_target="tpu_custom_call", output_to_operand_aliasing={{1}: (6, {}), {2}: (7, {}), {3}: (8, {})} | custom-call | flops 402653184 | bytes 8388608 | tf_op jit(solution)/shard_map/chain_step/pallas_call | solution.py:69
  94.7 58.3 %collective-permute-start.11 = (bf16[48,2048]{1,0:T(8,128)(2,1)S(1)}, bf16[48,2048]{1,0:T(8,128)(2,1)S(1)}, u32[]{:S(2)}, u32[]{:S(2)}) collective-permute-start(bf16[48,2048]{1,0:T(8,128)(2,1)S(1)} %get-tuple-element.216), channel_id=1, source_target_pairs={{160,144},{176,160},{192,176},{208,192},{224,208},{240,224},{161,1... | collective-permute-start | bytes 589832 | tf_op jit(solution)/shard_map/ppermute | solution.py:217
  153.1 15.9 %collective-permute-start.10 = (bf16[48,2048]{1,0:T(8,128)(2,1)S(1)}, bf16[48,2048]{1,0:T(8,128)(2,1)S(1)}, u32[]{:S(2)}, u32[]{:S(2)}) collective-permute-start(bf16[48,2048]{1,0:T(8,128)(2,1)S(1)} %get-tuple-element.215), channel_id=1, source_target_pairs={{160,144},{176,160},{192,176},{208,192},{224,208},{240,224},{161,1... | collective-permute-start | bytes 589832 | tf_op jit(solution)/shard_map/ppermute | solution.py:217
  169.0 15.9 %collective-permute-start.13 = (bf16[48,2048]{1,0:T(8,128)(2,1)S(1)}, bf16[48,2048]{1,0:T(8,128)(2,1)S(1)}, u32[]{:S(2)}, u32[]{:S(2)}) collective-permute-start(bf16[48,2048]{1,0:T(8,128)(2,1)S(1)} %get-tuple-element.224), channel_id=1, source_target_pairs={{144,128},{160,144},{176,160},{192,176},{208,192},{224,208},{145,1... | collective-permute-start | bytes 589832 | tf_op jit(solution)/shard_map/ppermute | solution.py:217
  185.0 15.9 %collective-permute-start.12 = (bf16[48,2048]{1,0:T(8,128)(2,1)S(1)}, bf16[48,2048]{1,0:T(8,128)(2,1)S(1)}, u32[]{:S(2)}, u32[]{:S(2)}) collective-permute-start(bf16[48,2048]{1,0:T(8,128)(2,1)S(1)} %get-tuple-element.223), channel_id=1, source_target_pairs={{144,128},{160,144},{176,160},{192,176},{208,192},{224,208},{145,1... | collective-permute-start | bytes 589832 | tf_op jit(solution)/shard_map/ppermute | solution.py:217
  200.9 15.9 %collective-permute-start.15 = (bf16[48,2048]{1,0:T(8,128)(2,1)S(1)}, bf16[48,2048]{1,0:T(8,128)(2,1)S(1)}, u32[]{:S(2)}, u32[]{:S(2)}) collective-permute-start(bf16[48,2048]{1,0:T(8,128)(2,1)S(1)} %get-tuple-element.232), channel_id=1, source_target_pairs={{128,112},{144,128},{160,144},{176,160},{192,176},{208,192},{129,1... | collective-permute-start | bytes 589832 | tf_op jit(solution)/shard_map/ppermute | solution.py:217
  223.7 3.8 chain_step.66
  231.5 56.8 %collective-permute-done.27.recv = bf16[48,2048]{1,0:T(8,128)(2,1)S(1)} collective-permute-done((bf16[48,2048]{1,0:T(8,128)(2,1)S(1)}, bf16[48,2048]{1,0:T(8,128)(2,1)S(1)}, u32[]{:S(2)}, u32[]{:S(2)}) %collective-permute-start.27) | collective-permute-done | bytes 196640 | tf_op jit(solution)/shard_map/ppermute | solution.py:217
  297.8 5.3 %collective-permute-done.29.recv = bf16[48,2048]{1,0:T(8,128)(2,1)S(1)} collective-permute-done((bf16[48,2048]{1,0:T(8,128)(2,1)S(1)}, bf16[48,2048]{1,0:T(8,128)(2,1)S(1)}, u32[]{:S(2)}, u32[]{:S(2)}) %collective-permute-start.29) | collective-permute-done | bytes 196640 | tf_op jit(solution)/shard_map/ppermute | solution.py:217
  308.7 3.0 chain_step.73
  313.7 4.0 collective-permute-done.31.recv
  327.6 4.7 collective-permute-done.33.recv
  341.8 5.9 %collective-permute-done.35.recv = bf16[48,2048]{1,0:T(8,128)(2,1)S(1)} collective-permute-done((bf16[48,2048]{1,0:T(8,128)(2,1)S(1)}, bf16[48,2048]{1,0:T(8,128)(2,1)S(1)}, u32[]{:S(2)}, u32[]{:S(2)}) %collective-permute-start.35) | collective-permute-done | bytes 196640 | tf_op jit(solution)/shard_map/ppermute | solution.py:217
  352.4 2.8 chain_step.79
  358.0 3.0 chain_step.80
  365.6 4.2 collective-permute-start.38
  371.8 3.3 collective-permute-done.39.recv
  376.4 9.0 %finish.1 = (bf16[2048,2048]{1,0:T(8,128)(2,1)}, bf16[576,2048]{1,0:T(8,128)(2,1)}, f32[1,2048]{1,0:T(1,128)S(1)}) custom-call(bf16[2048,576]{1,0:T(8,128)(2,1)S(1)} %fusion.3.normed_t, bf16[576,2048]{1,0:T(8,128)(2,1)S(1)} %get-tuple-element.335.grads, bf16[576,2048]{1,0:T(8,128)(2,1)S(1)} %get-tuple-element.336.din, f32[8,2048]{1,0:T(8,128)S(1)} %get-tuple-element.337.acc), custom_call_target="tpu_custom_call" | custom-call | flops 4831838208 | bytes 8388608 | tf_op jit(solution)/shard_map/finish/pallas_call | solution.py:117
  385.4 28.7 %psum.7 = f32[1,2048]{1,0:T(1,128)} all-reduce(f32[1,2048]{1,0:T(1,128)S(1)} %get-tuple-element.340), channel_id=1, replica_groups=mesh['section'=16,'fsdp'=16] {'fsdp'}, use_global_device_ids=true, to_apply=%region_3.0 | all-reduce | flops 2048 | bytes 16384 | tf_op jit(solution)/shard_map/psum | solution.py:220
  414.1 49.9 %reduce-scatter.2.cloned.1.call-done = bf16[128,2048]{1,0:T(8,128)(2,1)} async-done(((bf16[2048,2048]{1,0:T(8,128)(2,1)}), bf16[128,2048]{1,0:T(8,128)(2,1)}) %reduce-scatter.2.cloned.1.call-update) | async-done | bytes 524304 | tf_op jit(solution)/shard_map/reduce_scatter | solution.py:221
  (150 shorter events, 79.3 us)
Async XLA Ops:
  7.2 60.0 %all-gather.3.cloned.1.call-start = ((), (), s32[]{:S(2)}) async-start(), calls=%async_computation.2 | async-start | bytes 8912896 | tf_op jit(solution)/shard_map/all_gather | solution.py:186
  7.9 456.0 %reduce-scatter.2.cloned.1.call-start = ((), (), s32[]{:S(2)}) async-start(), calls=%async_computation.1 | async-start | bytes 8912896 | tf_op jit(solution)/shard_map/reduce_scatter | solution.py:221
  85.0 68.0 %collective-permute-start.8 = (bf16[48,2048]{1,0:T(8,128)(2,1)S(1)}, bf16[48,2048]{1,0:T(8,128)(2,1)S(1)}, u32[]{:S(2)}, u32[]{:S(2)}) collective-permute-start(bf16[48,2048]{1,0:T(8,128)(2,1)S(1)} %get-tuple-element.207), channel_id=1, source_target_pairs={{176,160},{192,176},{208,192},{224,208},{240,224},{177,161},{193,1... | collective-permute-start | bytes 589832 | tf_op jit(solution)/shard_map/ppermute | solution.py:217
  94.7 74.3 %collective-permute-start.11 = (bf16[48,2048]{1,0:T(8,128)(2,1)S(1)}, bf16[48,2048]{1,0:T(8,128)(2,1)S(1)}, u32[]{:S(2)}, u32[]{:S(2)}) collective-permute-start(bf16[48,2048]{1,0:T(8,128)(2,1)S(1)} %get-tuple-element.216), channel_id=1, source_target_pairs={{160,144},{176,160},{192,176},{208,192},{224,208},{240,224},{161,1... | collective-permute-start | bytes 589832 | tf_op jit(solution)/shard_map/ppermute | solution.py:217
  153.1 31.9 %collective-permute-start.10 = (bf16[48,2048]{1,0:T(8,128)(2,1)S(1)}, bf16[48,2048]{1,0:T(8,128)(2,1)S(1)}, u32[]{:S(2)}, u32[]{:S(2)}) collective-permute-start(bf16[48,2048]{1,0:T(8,128)(2,1)S(1)} %get-tuple-element.215), channel_id=1, source_target_pairs={{160,144},{176,160},{192,176},{208,192},{224,208},{240,224},{161,1... | collective-permute-start | bytes 589832 | tf_op jit(solution)/shard_map/ppermute | solution.py:217
  169.0 31.9 %collective-permute-start.13 = (bf16[48,2048]{1,0:T(8,128)(2,1)S(1)}, bf16[48,2048]{1,0:T(8,128)(2,1)S(1)}, u32[]{:S(2)}, u32[]{:S(2)}) collective-permute-start(bf16[48,2048]{1,0:T(8,128)(2,1)S(1)} %get-tuple-element.224), channel_id=1, source_target_pairs={{144,128},{160,144},{176,160},{192,176},{208,192},{224,208},{145,1... | collective-permute-start | bytes 589832 | tf_op jit(solution)/shard_map/ppermute | solution.py:217
  185.0 31.9 %collective-permute-start.12 = (bf16[48,2048]{1,0:T(8,128)(2,1)S(1)}, bf16[48,2048]{1,0:T(8,128)(2,1)S(1)}, u32[]{:S(2)}, u32[]{:S(2)}) collective-permute-start(bf16[48,2048]{1,0:T(8,128)(2,1)S(1)} %get-tuple-element.223), channel_id=1, source_target_pairs={{144,128},{160,144},{176,160},{192,176},{208,192},{224,208},{145,1... | collective-permute-start | bytes 589832 | tf_op jit(solution)/shard_map/ppermute | solution.py:217
  200.9 16.6 %collective-permute-start.15 = (bf16[48,2048]{1,0:T(8,128)(2,1)S(1)}, bf16[48,2048]{1,0:T(8,128)(2,1)S(1)}, u32[]{:S(2)}, u32[]{:S(2)}) collective-permute-start(bf16[48,2048]{1,0:T(8,128)(2,1)S(1)} %get-tuple-element.232), channel_id=1, source_target_pairs={{128,112},{144,128},{160,144},{176,160},{192,176},{208,192},{129,1... | collective-permute-start | bytes 589832 | tf_op jit(solution)/shard_map/ppermute | solution.py:217
  223.0 5.1 %collective-permute-start.22 = (bf16[48,2048]{1,0:T(8,128)(2,1)S(1)}, bf16[48,2048]{1,0:T(8,128)(2,1)S(1)}, u32[]{:S(2)}, u32[]{:S(2)}) collective-permute-start(bf16[48,2048]{1,0:T(8,128)(2,1)S(1)} %get-tuple-element.263), channel_id=1, source_target_pairs={{64,48},{80,64},{96,80},{112,96},{128,112},{144,128},{65,49},{81,6... | collective-permute-start | bytes 589832 | tf_op jit(solution)/shard_map/ppermute | solution.py:217
  228.1 2.0 collective-permute-start.24
  228.9 59.5 %collective-permute-start.27 = (bf16[48,2048]{1,0:T(8,128)(2,1)S(1)}, bf16[48,2048]{1,0:T(8,128)(2,1)S(1)}, u32[]{:S(2)}, u32[]{:S(2)}) collective-permute-start(bf16[48,2048]{1,0:T(8,128)(2,1)S(1)} %get-tuple-element.280), channel_id=1, source_target_pairs={{32,16},{48,32},{64,48},{80,64},{96,80},{112,96},{33,17},{49,33},{... | collective-permute-start | bytes 589832 | tf_op jit(solution)/shard_map/ppermute | solution.py:217
  230.2 62.9 %collective-permute-start.26 = (bf16[48,2048]{1,0:T(8,128)(2,1)S(1)}, bf16[48,2048]{1,0:T(8,128)(2,1)S(1)}, u32[]{:S(2)}, u32[]{:S(2)}) collective-permute-start(bf16[48,2048]{1,0:T(8,128)(2,1)S(1)} %get-tuple-element.279), channel_id=1, source_target_pairs={{32,16},{48,32},{64,48},{80,64},{96,80},{112,96},{33,17},{49,33},{... | collective-permute-start | bytes 589832 | tf_op jit(solution)/shard_map/ppermute | solution.py:217
  291.1 11.9 %collective-permute-start.29 = (bf16[48,2048]{1,0:T(8,128)(2,1)S(1)}, bf16[48,2048]{1,0:T(8,128)(2,1)S(1)}, u32[]{:S(2)}, u32[]{:S(2)}) collective-permute-start(bf16[48,2048]{1,0:T(8,128)(2,1)S(1)} %get-tuple-element.288), channel_id=1, source_target_pairs={{16,0},{32,16},{48,32},{64,48},{80,64},{96,80},{17,1},{33,17},{49,... | collective-permute-start | bytes 589832 | tf_op jit(solution)/shard_map/ppermute | solution.py:217
  295.9 12.9 %collective-permute-start.28 = (bf16[48,2048]{1,0:T(8,128)(2,1)S(1)}, bf16[48,2048]{1,0:T(8,128)(2,1)S(1)}, u32[]{:S(2)}, u32[]{:S(2)}) collective-permute-start(bf16[48,2048]{1,0:T(8,128)(2,1)S(1)} %get-tuple-element.287), channel_id=1, source_target_pairs={{16,0},{32,16},{48,32},{64,48},{80,64},{96,80},{17,1},{33,17},{49,... | collective-permute-start | bytes 589832 | tf_op jit(solution)/shard_map/ppermute | solution.py:217
  305.8 11.8 %collective-permute-start.31 = (bf16[48,2048]{1,0:T(8,128)(2,1)S(1)}, bf16[48,2048]{1,0:T(8,128)(2,1)S(1)}, u32[]{:S(2)}, u32[]{:S(2)}) collective-permute-start(bf16[48,2048]{1,0:T(8,128)(2,1)S(1)} %get-tuple-element.296), channel_id=1, source_target_pairs={{16,0},{32,16},{48,32},{64,48},{80,64},{17,1},{33,17},{49,33},{65,... | collective-permute-start | bytes 589832 | tf_op jit(solution)/shard_map/ppermute | solution.py:217
  311.7 11.1 %collective-permute-start.30 = (bf16[48,2048]{1,0:T(8,128)(2,1)S(1)}, bf16[48,2048]{1,0:T(8,128)(2,1)S(1)}, u32[]{:S(2)}, u32[]{:S(2)}) collective-permute-start(bf16[48,2048]{1,0:T(8,128)(2,1)S(1)} %get-tuple-element.295), channel_id=1, source_target_pairs={{16,0},{32,16},{48,32},{64,48},{80,64},{17,1},{33,17},{49,33},{65,... | collective-permute-start | bytes 589832 | tf_op jit(solution)/shard_map/ppermute | solution.py:217
  320.4 11.9 %collective-permute-start.33 = (bf16[48,2048]{1,0:T(8,128)(2,1)S(1)}, bf16[48,2048]{1,0:T(8,128)(2,1)S(1)}, u32[]{:S(2)}, u32[]{:S(2)}) collective-permute-start(bf16[48,2048]{1,0:T(8,128)(2,1)S(1)} %get-tuple-element.304), channel_id=1, source_target_pairs={{16,0},{32,16},{48,32},{64,48},{17,1},{33,17},{49,33},{65,49},{18,... | collective-permute-start | bytes 589832 | tf_op jit(solution)/shard_map/ppermute | solution.py:217
  325.7 11.4 %collective-permute-start.32 = (bf16[48,2048]{1,0:T(8,128)(2,1)S(1)}, bf16[48,2048]{1,0:T(8,128)(2,1)S(1)}, u32[]{:S(2)}, u32[]{:S(2)}) collective-permute-start(bf16[48,2048]{1,0:T(8,128)(2,1)S(1)} %get-tuple-element.303), channel_id=1, source_target_pairs={{16,0},{32,16},{48,32},{64,48},{17,1},{33,17},{49,33},{65,49},{18,... | collective-permute-start | bytes 589832 | tf_op jit(solution)/shard_map/ppermute | solution.py:217
  335.1 12.6 %collective-permute-start.35 = (bf16[48,2048]{1,0:T(8,128)(2,1)S(1)}, bf16[48,2048]{1,0:T(8,128)(2,1)S(1)}, u32[]{:S(2)}, u32[]{:S(2)}) collective-permute-start(bf16[48,2048]{1,0:T(8,128)(2,1)S(1)} %get-tuple-element.312), channel_id=1, source_target_pairs={{16,0},{32,16},{48,32},{17,1},{33,17},{49,33},{18,2},{34,18},{50,3... | collective-permute-start | bytes 589832 | tf_op jit(solution)/shard_map/ppermute | solution.py:217
  339.8 12.6 %collective-permute-start.34 = (bf16[48,2048]{1,0:T(8,128)(2,1)S(1)}, bf16[48,2048]{1,0:T(8,128)(2,1)S(1)}, u32[]{:S(2)}, u32[]{:S(2)}) collective-permute-start(bf16[48,2048]{1,0:T(8,128)(2,1)S(1)} %get-tuple-element.311), channel_id=1, source_target_pairs={{16,0},{32,16},{48,32},{17,1},{33,17},{49,33},{18,2},{34,18},{50,3... | collective-permute-start | bytes 589832 | tf_op jit(solution)/shard_map/ppermute | solution.py:217
  350.5 7.6 %collective-permute-start.37 = (bf16[48,2048]{1,0:T(8,128)(2,1)S(1)}, bf16[48,2048]{1,0:T(8,128)(2,1)S(1)}, u32[]{:S(2)}, u32[]{:S(2)}) collective-permute-start(bf16[48,2048]{1,0:T(8,128)(2,1)S(1)} %get-tuple-element.320), channel_id=1, source_target_pairs={{16,0},{32,16},{17,1},{33,17},{18,2},{34,18},{19,3},{35,19},{20,4}... | collective-permute-start | bytes 589832 | tf_op jit(solution)/shard_map/ppermute | solution.py:217
  355.2 7.6 %collective-permute-start.36 = (bf16[48,2048]{1,0:T(8,128)(2,1)S(1)}, bf16[48,2048]{1,0:T(8,128)(2,1)S(1)}, u32[]{:S(2)}, u32[]{:S(2)}) collective-permute-start(bf16[48,2048]{1,0:T(8,128)(2,1)S(1)} %get-tuple-element.319), channel_id=1, source_target_pairs={{16,0},{32,16},{17,1},{33,17},{18,2},{34,18},{19,3},{35,19},{20,4}... | collective-permute-start | bytes 589832 | tf_op jit(solution)/shard_map/ppermute | solution.py:217
  365.6 10.1 %collective-permute-start.38 = (bf16[48,2048]{1,0:T(8,128)(2,1)S(1)}, bf16[48,2048]{1,0:T(8,128)(2,1)S(1)}, u32[]{:S(2)}, u32[]{:S(2)}) collective-permute-start(bf16[48,2048]{1,0:T(8,128)(2,1)S(1)} %get-tuple-element.327), channel_id=1, source_target_pairs={{16,0},{17,1},{18,2},{19,3},{20,4},{21,5},{22,6},{23,7},{24,8},{25... | collective-permute-start | bytes 589832 | tf_op jit(solution)/shard_map/ppermute | solution.py:217
  369.8 5.3 %collective-permute-start.39 = (bf16[48,2048]{1,0:T(8,128)(2,1)S(1)}, bf16[48,2048]{1,0:T(8,128)(2,1)S(1)}, u32[]{:S(2)}, u32[]{:S(2)}) collective-permute-start(bf16[48,2048]{1,0:T(8,128)(2,1)S(1)} %get-tuple-element.328), channel_id=1, source_target_pairs={{16,0},{17,1},{18,2},{19,3},{20,4},{21,5},{22,6},{23,7},{24,8},{25... | collective-permute-start | bytes 589832 | tf_op jit(solution)/shard_map/ppermute | solution.py:217
  (30 other events, 150.6 us)
Sparse Core Ops, SparseCore 0:
  9.9 57.2 all-gather.2
  385.5 78.3 reduce-scatter.1
